TPU v7x, 128 devices: a whole 4x4x4 slice. The times are simulated.
128 devices in a mesh: blk: 8 (over y_lo, x), vslab: 16 (over z, y_hi, core).
Axes of the slice: x: 4, y: 4 (y_hi: 2, y_lo: 2; y = y_hi * 2 + y_lo), z: 4, core: 2. Of those that a mesh axis runs over, the one named last changes fastest.
Arguments:
- amplitudes: float32 [1024, 128, 800], P('blk', 'vslab'), may hold values from -6 to 6
- integrals: float32 [128, 800, 4096], P('vslab', None, 'blk'), may hold values from -0.01953125 to 0.01953125
- ab_energy: float32 [4096], P('blk'), may hold values from 1 to 4
- ij_energy: float32 [1024], replicated, may hold values from -4 to -1
- block_size: int32 [32], replicated, may hold values from 1 to 95, as said below
- block_owner: int32 [32], replicated, may hold values from 0 to 15, as said below
Outputs:
- amplitude_new: float32 [1024, 12288], P(None, ('blk', 'vslab'))
Inputs may be any that keep to these rules, and one draw needn't show every extreme that they name: `block_size`: the blocks of one group fill its 512 pairs exactly; every owner holds at most 96 pairs, and one owner exactly 96. `block_owner`: every owner has two blocks.
All inputs are finite; a program needn't handle non-finite values.
Results may differ from a plain program's by a relative error of at most 0.00007.
Values sent between devices are 32-bit elements; how exact they have to be, the bound alone decides.
No kernel may reach another device: no remote copies, remote signals or barrier semaphores. Data moves between devices by JAX's collectives and lax.ppermute only.
A program may use at most 128 MiB of HBM per device.

v0:
```python
import jax
import jax.numpy as jnp
from jax import lax
from jax.sharding import PartitionSpec as P


def slot_tables(block_size, block_owner, rows, owners, cap):
    count = block_size.shape[0]
    order = jnp.arange(count, dtype=jnp.int32)
    before_me = order[None, :] < order[:, None]
    starts = jnp.sum(jnp.where(before_me, block_size[None, :], 0), axis=1)
    same = block_owner[:, None] == block_owner[None, :]
    earlier = before_me
    before = jnp.sum(jnp.where(same & earlier, block_size[None, :], 0), axis=1)
    owner_hot = block_owner[:, None] == jnp.arange(owners, dtype=jnp.int32)[None, :]
    load = jnp.sum(jnp.where(owner_hot, block_size[:, None], 0), axis=0)
    owner_ids = jnp.arange(owners, dtype=jnp.int32)
    owner_start = jnp.sum(
        jnp.where(owner_ids[None, :] < owner_ids[:, None], load[None, :], 0), axis=1
    )
    block_base = jnp.sum(jnp.where(owner_hot, owner_start[None, :], 0), axis=1)
    shift_by = block_base + before - starts
    row_ids = jnp.arange(rows, dtype=jnp.int32)
    inside = (row_ids[:, None] >= starts[None, :]) & (
        row_ids[:, None] < (starts + block_size)[None, :]
    )
    position = jnp.sum(jnp.where(inside, shift_by[None, :], 0), axis=1) + row_ids
    perm = jnp.zeros((rows,), jnp.int32).at[position].set(row_ids)
    slot_ids = jnp.arange(cap, dtype=jnp.int32)
    valid = slot_ids[None, :] < load[:, None]
    index = jnp.minimum(owner_start[:, None] + slot_ids[None, :], rows - 1)
    source = perm[index]
    return (perm, owner_start, load, source, valid)


def on_device(amplitudes, integrals, ab_energy, ij_energy, block_size, block_owner):
    owners = lax.axis_size("vslab")
    rows = integrals.shape[2]
    cap = 3 * rows // owners
    v_matrix = integrals.reshape(-1, rows)
    t_tile = amplitudes.reshape(amplitudes.shape[0], -1)
    ladder = jnp.dot(
        lax.all_gather(t_tile, "blk", axis=0, tiled=True),
        v_matrix,
        precision=lax.Precision.HIGHEST,
        preferred_element_type=jnp.float32,
    )
    perm, owner_start, load, source, valid = slot_tables(block_size, block_owner, rows, owners, cap)
    mine = lax.axis_index("vslab")
    my_source = lax.dynamic_index_in_dim(source, mine, 0, keepdims=False)
    my_valid = lax.dynamic_index_in_dim(valid, mine, 0, keepdims=False)
    packed = jnp.take(ladder, source.reshape(-1), axis=1)
    packed = jnp.where(valid.reshape(1, -1), packed, 0.0).reshape(ladder.shape[0], owners, cap)
    received = lax.all_to_all(packed, "vslab", split_axis=1, concat_axis=1, tiled=True)
    summed = jnp.sum(received, axis=1)
    denom = jnp.take(ab_energy, my_source)[None, :] - ij_energy[:, None]
    return jnp.where(my_valid[None, :], summed / denom, 0.0)


def solution(mesh):
    placed = (P("blk", "vslab", None), P("vslab", None, "blk"), P("blk"), P(), P(), P())
    return jax.shard_map(
        on_device, mesh=mesh, in_specs=placed, out_specs=P(None, ("blk", "vslab")), check_vma=False
    )
```

profile of v0, /device:TPU:1, one launch (start us, length us, event | category | flops | bytes accessed | tf_op | source)
XLA Modules:
  0.0 425.9 jit_solution(9916567833174694342)
XLA Ops:
  6.5 0.0 copy-start
  6.5 0.0 all-gather.2.cloned.1.call-start
  6.5 0.7 all-gather.2.cloned.1.call-update
  7.3 0.8 select_reduce_fusion.5
  8.0 0.1 select_reduce_fusion.4
  8.2 0.1 compare_select_fusion.2
  8.2 0.1 reshape.187
  8.3 0.8 select_reduce_fusion.3
  9.1 0.9 select_reduce_fusion.1
  10.0 0.7 fusion.7
  10.6 0.1 select_reduce_fusion
  10.8 2.4 scatter_custom_fusion
  13.2 9.5 %gather_fusion = s32[1536]{0:T(1024)S(1)} fusion(s32[512]{0:T(512)S(1)} %scatter_custom_fusion, s32[2048]{0:T(1024)S(1)} %pad_clamp_fusion.1), kind=kCustom, calls=%fused_computation | custom fusion | bytes 18432 | tf_op jit(solution)/shard_map/gather | solution.py:32
  22.7 0.1 reshape.186
  22.8 0.1 iota_compare_fusion.5
  22.9 251.6 %all-gather.2.cloned.1.call-done = f32[1024,6400]{0,1:T(8,128)} async-done(((f32[128,6400]{0,1:T(8,128)}), f32[1024,6400]{0,1:T(8,128)}) %all-gather.2.cloned.1.call-update) | async-done | bytes 26214416 | tf_op jit(solution)/shard_map/all_gather | solution.py:43
  274.5 45.6 %fusion.8 = f32[1024,512]{0,1:T(8,128)S(1)} fusion(f32[1024,6400]{0,1:T(8,128)} %all-gather.2.cloned.1.call-done, f32[6400,512]{1,0:T(8,128)} %bitcast.27), kind=kOutput, calls=%fused_computation.40 | convolution fusion | flops 40265318400 | bytes 41418752 | tf_op jit(solution)/shard_map/dot_general | solution.py:42
  320.0 5.8 %gather_fusion.1 = f32[1536,1024]{1,0:T(8,128)} fusion(f32[1024,512]{0,1:T(8,128)S(1)} %fusion.8, s32[2048]{0:T(1024)S(1)} %pad_clamp_fusion), kind=kCustom, calls=%fused_computation.1 | custom fusion | bytes 12589056 | tf_op jit(solution)/shard_map/jit(_take)/gather | solution.py:52
  325.9 4.9 %select_select_fusion = f32[1024,16,96]{0,2,1:T(8,128)} fusion(f32[1024,16,96]{0,2,1:T(8,128)} %bitcast.23, pred[16,96]{1,0:T(8,128)(4,1)S(1)} %get-tuple-element.10, pred[16,96]{1,0:T(8,128)(4,1)S(1)} %get-tuple-element.9), kind=kLoop, calls=%fused_computation.4 | loop fusion | flops 3145728 | bytes 12585984 | tf_op jit(solution)/shard_map/jit(_where)/select_n | solution.py:53
  330.8 10.4 %all-to-all-start = ((f32[1024,16,96]{0,2,1:T(8,128)}), f32[1024,16,96]{0,2,1:T(8,128)}, u32[]{:S(2)}, u32[]{:S(2)}) async-start(f32[1024,16,96]{0,2,1:T(8,128)} %select_select_fusion), calls=%async_computation | async-start | bytes 12582912 | tf_op jit(solution)/shard_map/all_to_all | solution.py:54
  341.2 0.0 copy-start.1
  341.3 0.0 copy-done
  341.3 1.3 gather_fusion.2
  342.6 72.2 %all-to-all-done = f32[1024,16,96]{0,2,1:T(8,128)} async-done(((f32[1024,16,96]{0,2,1:T(8,128)}), f32[1024,16,96]{0,2,1:T(8,128)}, u32[]{:S(2)}, u32[]{:S(2)}) %all-to-all-start) | async-done | bytes 6291488 | tf_op jit(solution)/shard_map/all_to_all | solution.py:54
  414.8 3.4 reduce_sum.72
  418.2 0.0 copy-done.1
  418.2 0.9 divide_select_fusion
  (9 shorter events, 0.1 us)
Async XLA Ops:
  6.5 334.7 %copy-start = (f32[512]{0:T(512)S(1)}, f32[512]{0:T(512)}, u32[]{:S(2)}) copy-start(f32[512]{0:T(512)} %param.8) | copy-start | bytes 6148
  6.5 267.9 %all-gather.2.cloned.1.call-start = ((), (), s32[]{:S(2)}) async-start(), calls=%async_computation.1 | async-start | bytes 29491200 | tf_op jit(solution)/shard_map/all_gather | solution.py:43
  330.8 84.0 %all-to-all-start = ((f32[1024,16,96]{0,2,1:T(8,128)}), f32[1024,16,96]{0,2,1:T(8,128)}, u32[]{:S(2)}, u32[]{:S(2)}) async-start(f32[1024,16,96]{0,2,1:T(8,128)} %select_select_fusion), calls=%async_computation | async-start | bytes 12582912 | tf_op jit(solution)/shard_map/all_to_all | solution.py:54
  341.2 76.9 %copy-start.1 = (f32[1024]{0:T(1024)S(1)}, f32[1024]{0:T(1024)}, u32[]{:S(2)}) copy-start(f32[1024]{0:T(1024)} %param.9) | copy-start | bytes 12292
Sparse Core Ops, SparseCore 0:
  8.9 265.4 all-gather.1
where the time goes:
time: 426 us
  waiting for transfers between devices  324 us (76%)
  matrix products  45.6 us (11%)
  local copies, waits for them, and re-layouts  19.2 us (5%)
  between operations  13.5 us (3%)
  other arithmetic  12.7 us (3%)
  starting transfers between devices  10.4 us (2%)
    all_gather x1, waiting for transfers between devices, on_device(): lax.all_gather(t_tile, 'blk', axis=0, tiled=True)  252 us
    all_to_all x1, waiting for transfers between devices, on_device(): lax.all_to_all(packed, 'vslab', split_axis=1, concat_axis=1, tiled=True)  72.2 us
    dot_general x1, matrix products, on_device(): jnp.dot(lax.all_gather(t_tile, 'blk', axis=0, tiled=True), v_matrix, prec...  45.6 us
    all_to_all x1, starting transfers between devices, on_device(): lax.all_to_all(packed, 'vslab', split_axis=1, concat_axis=1, tiled=True)  10.4 us
    gather x2, local copies, waits for them, and re-layouts, slot_tables(): source = perm[index]  9.54 us
  transfers between devices with their start and end apart: 2, of which 2 were waited for; matrix products, arithmetic and copies ran while one was open for 4% of the time, Pallas kernels for 0%

commit v1 on v0

--- a/solution.py
+++ b/solution.py
@@ -39,8 +39,20 @@
     cap = 3 * rows // owners
     v_matrix = integrals.reshape(-1, rows)
     t_tile = amplitudes.reshape(amplitudes.shape[0], -1)
+
+    def deliver_heads_all(content):
+        return jnp.concatenate(
+            lax.all_to_all(
+                jnp.stack([content] * lax.axis_size("blk"), axis=0),
+                axis_name="blk",
+                split_axis=0,
+                concat_axis=0,
+            ),
+            axis=0,
+        )
+
     ladder = jnp.dot(
-        lax.all_gather(t_tile, "blk", axis=0, tiled=True),
+        deliver_heads_all(t_tile),
         v_matrix,
         precision=lax.Precision.HIGHEST,
         preferred_element_type=jnp.float32,

time: 426 us -> 557 us (1.31)
  the two profiles are of different devices: /device:TPU:1 before, /device:TPU:6 now
where the time goes in v1:
time: 557 us; the launch traced here: 556 us
  waiting for transfers between devices  452 us (81%)
  matrix products  45.8 us (8%)
  local copies, waits for them, and re-layouts  33.7 us (6%)
  starting transfers between devices  15.2 us (3%)
  other arithmetic  10 us (2%)
    all_to_all x1, waiting for transfers between devices, deliver_heads_all(): lax.all_to_all(jnp.stack([content] * lax.axis_size('blk'), axis=0), axis_...  379 us
    all_to_all x1, waiting for transfers between devices, on_device(): lax.all_to_all(packed, 'vslab', split_axis=1, concat_axis=1, tiled=True)  73 us
    dot_general x1, matrix products, on_device(): jnp.dot(deliver_heads_all(t_tile), v_matrix, precision=lax.Precision.HIGH...  45.8 us
    another operation x2, local copies, waits for them, and re-layouts, deliver_heads_all(): jnp.stack([content] * lax.axis_size('blk'), axis=0)  14.3 us
  transfers between devices with their start and end apart: 2, of which 2 were waited for; matrix products, arithmetic and copies ran while one was open for 3% of the time, Pallas kernels for 0%

profile of v1, /device:TPU:6, one launch (start us, length us, event | category | flops | bytes accessed | tf_op | source)
XLA Modules:
  0.0 556.5 jit_solution(18389241839099485380)
XLA Ops:
  0.0 0.0 copy-start
  0.0 3.4 copy.11
  3.4 10.9 %stack.3 = f32[8,128,6400]{2,1,0:T(8,128)} broadcast(f32[128,6400]{1,0:T(8,128)S(1)} %copy.11), dimensions={1,2} | broadcast | bytes 29491200 | tf_op jit(solution)/shard_map/stack | solution.py:46
  14.3 0.0 copy-start.2
  14.3 0.0 copy-start.3
  14.3 6.9 %all-to-all-start = ((f32[8,128,6400]{2,1,0:T(8,128)}), f32[8,128,6400]{2,1,0:T(8,128)}, u32[]{:S(2)}, u32[]{:S(2)}) async-start(f32[8,128,6400]{2,1,0:T(8,128)} %stack.3), calls=%async_computation | async-start | bytes 52428800 | tf_op jit(solution)/shard_map/all_to_all | solution.py:45
  21.2 0.0 copy-done.2
  21.2 0.0 copy-done.3
  21.2 0.1 select_reduce_fusion.5
  21.3 0.1 select_reduce_fusion.4
  21.5 0.1 compare_select_fusion.2
  21.5 0.1 reshape.189
  21.6 0.1 select_reduce_fusion.3
  21.7 0.2 select_reduce_fusion.1
  21.9 0.1 select_reduce_fusion
  22.0 2.6 scatter_custom_fusion
  24.7 9.5 %gather_fusion = s32[1536]{0:T(1024)S(1)} fusion(s32[512]{0:T(512)S(1)} %scatter_custom_fusion, s32[2048]{0:T(1024)S(1)} %pad_clamp_fusion.1), kind=kCustom, calls=%fused_computation | custom fusion | bytes 18432 | tf_op jit(solution)/shard_map/gather | solution.py:32
  34.1 0.1 reshape.188
  34.2 0.1 iota_compare_fusion.5
  34.3 378.6 %all-to-all-done = f32[8,128,6400]{2,1,0:T(8,128)} async-done(((f32[8,128,6400]{2,1,0:T(8,128)}), f32[8,128,6400]{2,1,0:T(8,128)}, u32[]{:S(2)}, u32[]{:S(2)}) %all-to-all-start) | async-done | bytes 26214432 | tf_op jit(solution)/shard_map/all_to_all | solution.py:45
  412.9 45.8 %fusion.8 = f32[1024,512]{0,1:T(8,128)S(1)} fusion(f32[1024,6400]{1,0:T(8,128)} %bitcast.4, f32[6400,512]{1,0:T(8,128)} %bitcast.28), kind=kOutput, calls=%fused_computation.40 | convolution fusion | flops 40265318400 | bytes 41418752 | tf_op jit(solution)/shard_map/dot_general | solution.py:54
  458.7 5.8 %gather_fusion.1 = f32[1536,1024]{1,0:T(8,128)} fusion(f32[1024,512]{0,1:T(8,128)S(1)} %fusion.8, s32[2048]{0:T(1024)S(1)} %pad_clamp_fusion), kind=kCustom, calls=%fused_computation.1 | custom fusion | bytes 12589056 | tf_op jit(solution)/shard_map/jit(_take)/gather | solution.py:64
  464.6 4.9 select_select_fusion
  469.5 8.3 %all-to-all-start.1 = ((f32[1024,16,96]{0,2,1:T(8,128)}), f32[1024,16,96]{0,2,1:T(8,128)}, u32[]{:S(2)}, u32[]{:S(2)}) async-start(f32[1024,16,96]{0,2,1:T(8,128)} %select_select_fusion), calls=%async_computation.1 | async-start | bytes 12582912 | tf_op jit(solution)/shard_map/all_to_all | solution.py:66
  477.9 0.0 copy-start.1
  477.9 0.0 copy-done
  477.9 1.3 gather_fusion.2
  479.2 73.0 %all-to-all-done.1 = f32[1024,16,96]{0,2,1:T(8,128)} async-done(((f32[1024,16,96]{0,2,1:T(8,128)}), f32[1024,16,96]{0,2,1:T(8,128)}, u32[]{:S(2)}, u32[]{:S(2)}) %all-to-all-start.1) | async-done | bytes 6291488 | tf_op jit(solution)/shard_map/all_to_all | solution.py:66
  552.2 3.4 reduce_sum.72
  555.6 0.0 copy-done.1
  555.6 0.9 divide_select_fusion
  (10 shorter events, 0.1 us)
Async XLA Ops:
  0.0 477.9 %copy-start = (f32[512]{0:T(512)S(1)}, f32[512]{0:T(512)}, u32[]{:S(2)}) copy-start(f32[512]{0:T(512)} %param.8) | copy-start | bytes 6148
  14.3 6.9 %copy-start.2 = (s32[32]{0:T(128)S(1)}, s32[32]{0:T(128)}, u32[]{:S(2)}) copy-start(s32[32]{0:T(128)} %param.11) | copy-start | bytes 388
  14.3 6.9 %copy-start.3 = (s32[32]{0:T(128)S(1)}, s32[32]{0:T(128)}, u32[]{:S(2)}) copy-start(s32[32]{0:T(128)} %param.10) | copy-start | bytes 388
  14.3 398.6 %all-to-all-start = ((f32[8,128,6400]{2,1,0:T(8,128)}), f32[8,128,6400]{2,1,0:T(8,128)}, u32[]{:S(2)}, u32[]{:S(2)}) async-start(f32[8,128,6400]{2,1,0:T(8,128)} %stack.3), calls=%async_computation | async-start | bytes 52428800 | tf_op jit(solution)/shard_map/all_to_all | solution.py:45
  469.5 82.7 %all-to-all-start.1 = ((f32[1024,16,96]{0,2,1:T(8,128)}), f32[1024,16,96]{0,2,1:T(8,128)}, u32[]{:S(2)}, u32[]{:S(2)}) async-start(f32[1024,16,96]{0,2,1:T(8,128)} %select_select_fusion), calls=%async_computation.1 | async-start | bytes 12582912 | tf_op jit(solution)/shard_map/all_to_all | solution.py:66
  477.9 77.7 %copy-start.1 = (f32[1024]{0:T(1024)S(1)}, f32[1024]{0:T(1024)}, u32[]{:S(2)}) copy-start(f32[1024]{0:T(1024)} %param.9) | copy-start | bytes 12292
